TPU v7x, 256 devices: a whole 4x4x8 slice. The times are simulated.
256 devices in a mesh: wide: 64 (over z, x, core), narrow: 4 (over y).
Axes of the slice: x: 4, y: 4, z: 8, core: 2. Of those that a mesh axis runs over, the one named last changes fastest.
Arguments:
- panel: bfloat16 [196608, 3, 2048], P('wide', None, 'narrow'), may hold values from -0.013671875 to 0.013671875
- tail_samples: bfloat16 [196608, 256], P('wide'), may hold values from -6 to 6
- noise: float32 [3, 2048, 256], P(None, 'narrow'), may hold values from -6 to 6
- inner: float32 [3, 2048, 2048], P(None, 'wide', 'narrow'), may hold values from -0.125 to 0.125
- diag_inverse: float32 [3, 2048, 2048], P(None, 'narrow', 'wide'), as said below
Outputs:
- samples: float32 [3, 2048, 256], P(None, 'wide')
Inputs may be any that keep to these rules, and one draw needn't show every extreme that they name: `diag_inverse`: each block is lower triangular with its diagonal between 0.5 and 1.5.
All inputs are finite; a program needn't handle non-finite values.
Results may differ from a plain program's by a relative error of at most 0.0003.
Values sent between devices are 32-bit elements; how exact they have to be, the bound alone decides.
A program may use at most 64 MiB of HBM per device.

v0:
```python
import jax
import jax.numpy as jnp
from jax import lax
from jax.sharding import PartitionSpec as P

HI = lax.Precision.HIGHEST


def solve_block(inverse, remainder):
    return lax.psum(jnp.dot(inverse.T, remainder, precision=HI), "narrow")


def local(panel, tail_samples, noise, inner, diag_inverse):
    partial_value = jnp.einsum(
        "rkj,rs->kjs", panel, tail_samples, preferred_element_type=jnp.float32
    )
    tail_terms = lax.psum(partial_value, "wide")
    remain = noise - tail_terms
    x_two = solve_block(diag_inverse[2], remain[2])
    upd_one, upd_zero = lax.psum(
        (jnp.dot(inner[2].T, x_two, precision=HI), jnp.dot(inner[1].T, x_two, precision=HI)), "wide"
    )
    r_one = remain[1] - upd_one
    r_zero_part = remain[0] - upd_zero
    x_one = solve_block(diag_inverse[1], r_one)
    upd_last = lax.psum(jnp.dot(inner[0].T, x_one, precision=HI), "wide")
    x_zero = solve_block(diag_inverse[0], r_zero_part - upd_last)
    return jnp.stack([x_zero, x_one, x_two], axis=0)


def solution(mesh):
    placed = (
        P("wide", None, "narrow"),
        P("wide", None),
        P(None, "narrow", None),
        P(None, "wide", "narrow"),
        P(None, "narrow", "wide"),
    )
    return jax.shard_map(
        local, mesh=mesh, in_specs=placed, out_specs=P(None, "wide", None), check_vma=False
    )
```

profile of v0, /device:TPU:1, one launch (start us, length us, event | category | flops | bytes accessed | tf_op | source)
XLA Modules:
  0.0 629.5 jit_solution(14172696405584216778)
XLA Ops:
  6.5 0.0 copy-start
  6.5 1.4 copy-done
  7.9 7.5 %fusion = f32[3,512,256]{2,1,0:T(8,128)} fusion(bf16[3072,3,512]{2,0,1:T(8,128)(2,1)} %param.5, bf16[3072,256]{1,0:T(8,128)(2,1)S(1)} %copy-done), kind=kOutput, calls=%fused_computation | convolution fusion | flops 2415919104 | bytes 12582912 | tf_op jit(solution)/shard_map/rkj,rs->kjs/dot_general | solution.py:14
  15.4 0.0 all-reduce.5.cloned.1.call-update
  15.4 0.0 copy-start.1
  15.5 0.0 all-reduce.7.cloned.1.call-start
  15.5 189.9 %all-reduce.5.cloned.1.call-done = f32[3,512,256]{2,1,0:T(8,128)} async-done(((f32[3,512,256]{2,1,0:T(8,128)}), f32[3,512,256]{2,1,0:T(8,128)}) %all-reduce.5.cloned.1.call-update) | async-done | bytes 1572880 | tf_op jit(solution)/shard_map/psum | solution.py:17
  205.4 2.1 sub.12
  207.5 1.2 convolution_bitcast_fusion.5
  208.7 13.3 %psum.50 = f32[32,256]{1,0:T(8,128)S(1)} all-reduce(f32[32,256]{1,0:T(8,128)S(1)} %convolution_bitcast_fusion.5), channel_id=1, replica_groups=mesh['wide'=64,'narrow'=4] {'narrow'}, use_global_device_ids=true, to_apply=%region_1.0 | all-reduce | flops 8192 | bytes 65536 | tf_op jit(solution)/shard_map/psum | solution.py:10
  222.0 0.0 copy-done.1
  222.1 1.4 convolution_bitcast_fusion.1
  223.5 0.0 all-reduce.7.cloned.1.call-update
  223.5 0.0 all-reduce.9.cloned.1.call-start
  223.6 1.4 convolution_bitcast_fusion.2
  225.0 181.0 %all-reduce.7.cloned.1.call-done = f32[512,256]{1,0:T(8,128)} async-done(((f32[512,256]{1,0:T(8,128)}), f32[512,256]{1,0:T(8,128)}) %all-reduce.7.cloned.1.call-update) | async-done | bytes 524304 | tf_op jit(solution)/shard_map/psum | solution.py:20
  406.0 1.4 convolution_bitcast_fusion.4
  407.5 13.4 %psum.53 = f32[32,256]{1,0:T(8,128)S(1)} all-reduce(f32[32,256]{1,0:T(8,128)S(1)} %convolution_bitcast_fusion.4), channel_id=1, replica_groups=mesh['wide'=64,'narrow'=4] {'narrow'}, use_global_device_ids=true, to_apply=%region_4.0 | all-reduce | flops 8192 | bytes 65536 | tf_op jit(solution)/shard_map/psum | solution.py:10
  420.8 1.4 convolution_bitcast_fusion
  422.3 0.0 all-reduce.9.cloned.1.call-update
  422.3 185.0 %all-reduce.9.cloned.1.call-done = (f32[512,256]{1,0:T(8,128)}, f32[512,256]{1,0:T(8,128)}) async-done(((f32[512,256]{1,0:T(8,128)}, f32[512,256]{1,0:T(8,128)}), (f32[512,256]{1,0:T(8,128)}, f32[512,256]{1,0:T(8,128)})) %all-reduce.9.cloned.1.call-update) | async-done | bytes 1048592 | tf_op jit(solution)/shard_map/psum | solution.py:26
  607.3 1.6 convolution_bitcast_fusion.3
  608.9 13.4 %psum.55 = f32[1,32,256]{2,1,0:T(8,128)S(1)} all-reduce(f32[1,32,256]{2,1,0:T(8,128)S(1)} %convolution_bitcast_fusion.3), channel_id=1, replica_groups=mesh['wide'=64,'narrow'=4] {'narrow'}, use_global_device_ids=true, to_apply=%region_6.0 | all-reduce | flops 8192 | bytes 65536 | tf_op jit(solution)/shard_map/psum | solution.py:10
  622.3 0.6 pad_maximum_fusion
  (1 shorter events, 0.0 us)
Async XLA Ops:
  6.5 1.4 copy-start
  6.5 198.9 %all-reduce.5.cloned.1.call-start = ((), (), s32[]{:S(2)}) async-start(), calls=%async_computation | async-start | bytes 3145728 | tf_op jit(solution)/shard_map/psum | solution.py:17
  15.4 206.6 %copy-start.1 = (f32[3,32,512]{2,1,0:T(8,128)S(1)}, f32[3,32,512]{2,1,0:T(8,128)}, u32[]{:S(2)}) copy-start(f32[3,32,512]{2,1,0:T(8,128)} %param.8) | copy-start | bytes 589828
  15.5 390.5 %all-reduce.7.cloned.1.call-start = ((), (), s32[]{:S(2)}) async-start(), calls=%async_computation.1 | async-start | bytes 1048576 | tf_op jit(solution)/shard_map/psum | solution.py:20
  223.5 383.8 %all-reduce.9.cloned.1.call-start = ((), (), s32[]{:S(2)}) async-start(), calls=%async_computation.2 | async-start | bytes 2097152 | tf_op jit(solution)/shard_map/psum | solution.py:26
Sparse Core Ops, SparseCore 0:
  15.6 189.8 all-reduce.4
  223.6 182.3 all-reduce.6
  422.4 184.8 all-reduce.8
where the time goes:
time: 634 us; the launch traced here: 629 us
  waiting for transfers between devices  556 us (88%)
  blocking collectives  40 us (6%)
  matrix products  16.1 us (3%)
  between operations  13.2 us (2%)
    psum x1, waiting for transfers between devices, local(): tail_terms = lax.psum(partial_value, 'wide')  190 us
    psum x1, waiting for transfers between devices, local(): upd_last = lax.psum(jnp.dot(inner[0].T, x_one, precision=HI), 'wide')  185 us
    psum x1, waiting for transfers between devices, local(): lax.psum((jnp.dot(inner[2].T, x_two, precision=HI), jnp.dot(inner[1].T, x...  181 us
    psum x3, blocking collectives, solve_block(): return lax.psum(jnp.dot(inverse.T, remainder, precision=HI), 'narrow')  40 us
  transfers between devices with their start and end apart: 3, of which 3 were waited for; matrix products, arithmetic and copies ran while one was open for 0% of the time, Pallas kernels for 0%

commit v1 on v0

v1 whole, which is shorter than its diff:
```python
import jax
import jax.numpy as jnp
from jax import lax
from jax.experimental import pallas as pl
from jax.experimental.pallas import tpu as pltpu
from jax.sharding import PartitionSpec as P

MESH = pl.DeviceIdType.MESH
NZ, NX, NY, NC = 8, 4, 4, 2
ROWS, DEPTH, COLS, S, PIECE = 3072, 1024, 512, 256, 32
PART = 128
GROUP = S // (NZ * NC)
F32, BF16 = jnp.float32, jnp.bfloat16
D2, L21, D1, L20, L10, D0 = range(6)
SOURCE = (("d", 2), ("i", 2), ("d", 1), ("i", 1), ("i", 0), ("d", 0))
PLAN = {
    "start": [(m, 0) for m in range(6)],
    "x2": [(D2, 1), (L21, 1)],
    "tails": [(D2, 2), (D1, 1)],
    "z2": [(L21, 2), (D2, 3)],
    "g2": [(D2, 4), (L21, 3), (D1, 2), (L20, 1), (D2, 5), (D2, 6)],
    "y2": [(L21, 4), (D1, 3), (L20, 2), (L10, 1), (L21, 5), (L21, 6)],
    "u1": [(D1, 4), (L20, 3), (L10, 2), (D0, 1), (D1, 5), (D1, 6)],
    "y1": [(L20, 4), (L10, 3), (D0, 2), (L20, 5), (L10, 4), (D0, 3), (L10, 5), (L20, 6), (L10, 6)],
    "u0": [(D0, 4), (D0, 5), (D0, 6)],
}


def halves(a):
    high = a.astype(BF16)
    return high, (a - high.astype(F32)).astype(BF16)


def kernel(
    panel, tail, noise, inner, diag, out,
    pan_v, ts_v, ts_t, noise_v, noise_t, part_t, half_in, half_sum, x_in, z_sum, z_in, right, grid, high, low,
    y_buf, u_buf, solved, out_in, flat,
    load_sem, own_sem, hs, hr, xs, xr, zs, zr, gs, gr, cs, cr, rs, rr, ss, sr, ys, yr, us, ur, os, orr, ps, pr,
):
    wide, y = lax.axis_index("wide"), lax.axis_index("narrow")
    z, x, c = wide // (NX * NC), (wide // NC) % NX, wide % NC
    way = 1 - 2 * c

    def at(z_to, x_to, c_to, y_to):
        return ((z_to * NX + x_to) * NC + c_to, y_to)

    def send(src, dst, send_sem, recv_sem, to):
        return pltpu.make_async_remote_copy(
            src_ref=src, dst_ref=dst, send_sem=send_sem, recv_sem=recv_sem, device_id=to, device_id_type=MESH
        )

    def zp(k):
        return (z + k + 2 * NZ) % NZ

    def xp(k):
        return (x + k + NX) % NX

    def yp(k):
        return (y + k + NY) % NY

    mate = at(z, x, 1 - c, y)
    partners = (
        [mate]
        + [at(zp(k), x, c, y) for k in range(1, NZ)]
        + [at(z, xp(k), c, y) for k in range(1, NX)]
        + [at(z, x, c, yp(k)) for k in range(1, NY)]
    )
    barrier = pltpu.get_barrier_semaphore()
    for to in partners:
        pl.semaphore_signal(barrier, inc=1, device_id=to, device_id_type=MESH)

    chunks = ROWS // DEPTH
    loads = {}
    count = 0
    for q in range(chunks):
        rows = pl.ds(q * DEPTH, DEPTH)
        for name, src, dst in (("ts", tail.at[rows], ts_v.at[rows]), ("p2", panel.at[2, rows], pan_v.at[2, rows])):
            loads[name, q] = pltpu.make_async_copy(src, dst, load_sem.at[count])
            loads[name, q].start()
            count += 1
    own = []
    for m, (kind, k) in enumerate(SOURCE):
        src = diag.at[k] if kind == "d" else inner.at[k]
        own.append(pltpu.make_async_copy(src, grid.at[m, z, c], own_sem.at[m]))
        own[-1].start()
    for k in (1, 0):
        for q in range(chunks):
            rows = pl.ds(q * DEPTH, DEPTH)
            loads[f"p{k}", q] = pltpu.make_async_copy(panel.at[k, rows], pan_v.at[k, rows], load_sem.at[count])
            loads[f"p{k}", q].start()
            count += 1
    loads["noise"] = pltpu.make_async_copy(
        noise.at[:, pl.ds(pl.multiple_of(x * PART, PART), PART), pl.ds(pl.multiple_of(c * PART, PART), PART)],
        noise_v, load_sem.at[count])
    loads["noise"].start()

    def multiply(k):
        for q in range(chunks):
            rows = pl.ds(q * DEPTH, DEPTH)
            if k == 2:
                loads["ts", q].wait()
                ts_t[:, q * DEPTH : (q + 1) * DEPTH] = ts_v[rows, :].T
            loads[f"p{k}", q].wait()
            term = jnp.dot(ts_t[:, q * DEPTH : (q + 1) * DEPTH], pan_v[k, rows, :], preferred_element_type=F32)
            if q == 0:
                part_t[k] = term
            else:
                part_t[k] += term

    def half_send(k):
        return send(part_t.at[k, pl.ds(pl.multiple_of((1 - c) * PART, PART), PART)], half_in.at[k], hs.at[k], hr.at[k], mate)

    def x_send(k, d):
        return send(half_sum.at[k, xp(d)], x_in.at[k, x], xs.at[k, d - 1], xr.at[k, d - 1], at(z, xp(d), c, y))

    def z_send(k, d):
        return send(z_sum.at[k, zp(d)], z_in.at[k, z], zs.at[k, d - 1], zr.at[k, d - 1], at(zp(d), x, c, y))

    def g_send(k, d):
        return send(right.at[k, x], right.at[k, x], gs.at[k, d - 1], gr.at[k, d - 1], at(z, xp(d), c, y))

    def half_to_x(k):
        half_send(k).wait_recv()
        both = part_t[k, pl.ds(pl.multiple_of(c * PART, PART), PART), :] + half_in[k]
        for i in range(NX):
            half_sum[k, i] = both[:, i * PART : (i + 1) * PART]
        for d in (2, 1, 3):
            x_send(k, d).start()

    def x_to_z(k):
        for d in (1, 3, 2):
            x_send(k, d).wait_recv()
        total = half_sum[k, x]
        for d in range(1, NX):
            total = total + x_in[k, xp(d)]
        z_sum[k] = total.reshape(NZ, GROUP, PART)
        for d in (4, 3, 5, 2, 6, 1, 7):
            z_send(k, d).start()

    def z_to_g(k):
        for d in range(1, NZ):
            z_send(k, d).wait_recv()
        total = z_sum[k, z]
        for d in range(1, NZ):
            total = total + z_in[k, zp(d)]
        right[k, x] = noise_t[k, z] - total
        for d in (2, 1, 3):
            g_send(k, d).start()

    def gathered(k):
        for d in (1, 3, 2):
            g_send(k, d).wait_recv()
        return jnp.concatenate([right[k, i] for i in range(NX)], axis=1)

    def c_send(m):
        return send(grid.at[m, z, c], grid.at[m, z, c], cs.at[m], cr.at[m], mate)

    def ring(m, s):
        if s < 4:
            piece = grid.at[m, zp(-(s - 1) * way)]
        else:
            piece = grid.at[m, zp(-3 * way), c]
        return send(piece, piece, rs.at[m, s - 1], rr.at[m, s - 1], at(zp(way), x, c, y))

    def share(m, s):
        piece = grid.at[m, zp(-s * way)] if s < 4 else grid.at[m, zp(-4 * way), c]
        return send(piece, piece, ss.at[m, s - 1], sr.at[m, s - 1], mate)

    def step(m, s):
        if s == 0:
            own[m].wait()
            c_send(m).start()
        elif s == 1:
            c_send(m).wait_recv()
            ring(m, 1).start()
        elif s < 5:
            ring(m, s - 1).wait_recv()
            ring(m, s).start()
            share(m, s - 1).start()
        elif s == 5:
            ring(m, 4).wait_recv()
            share(m, 4).start()
        else:
            for q in range(1, 5):
                share(m, q).wait_recv()
            for q in range(2):
                zs_ = slice(q * NZ // 2, (q + 1) * NZ // 2)
                rows = slice(q * COLS // 2, (q + 1) * COLS // 2)
                high[m, rows], low[m, rows] = halves(grid[m, zs_].reshape(COLS // 2, COLS))

    def pump(point):
        for m, s in PLAN[point]:
            step(m, s)

    def product(m, vector):
        dims = (((1,), (1,)), ((), ())) if SOURCE[m][0] == "d" else (((1,), (0,)), ((), ()))
        v_high, v_low = halves(vector)
        both = lax.dot_general(jnp.concatenate([v_high, v_low], axis=0), high[m], dims, preferred_element_type=F32)
        rest = lax.dot_general(v_high, low[m], dims, preferred_element_type=F32)
        return both[:GROUP] + both[GROUP:] + rest

    def y_send(k, d):
        return send(y_buf.at[k, y], y_buf.at[k, y], ys.at[k, d - 1], yr.at[k, d - 1], at(z, x, c, yp(d)))

    def y_start(k, term):
        y_buf[k, y] = term
        for d in (2, 1, 3):
            y_send(k, d).start()

    def y_end(k):
        for d in (1, 3, 2):
            y_send(k, d).wait_recv()
        total = (y_buf[k, 0] + y_buf[k, 1]) + (y_buf[k, 2] + y_buf[k, 3])
        return total

    def u_send(k, d):
        return send(u_buf.at[k, x], u_buf.at[k, x], us.at[k, d - 1], ur.at[k, d - 1], at(z, xp(d), c, y))

    def u_start(k, term):
        u_buf[k, x] = term
        for d in (2, 1, 3):
            u_send(k, d).start()

    def u_end(k):
        for d in (1, 3, 2):
            u_send(k, d).wait_recv()
        return (u_buf[k, 0] + u_buf[k, 1]) + (u_buf[k, 2] + u_buf[k, 3])

    def out_send(k, d):
        return send(
            solved.at[k, zp(d) // 2], out_in.at[k, c, z], os.at[k, d - 1], orr.at[k, d - 1], at(zp(d), x, c, y)
        )

    def out_share(k):
        return send(out_in.at[k, c], out_in.at[k, c], ps.at[k], pr.at[k], mate)

    def out_start(k, vector):
        for i in range(NX):
            solved[k, i] = vector[:, i * PART : (i + 1) * PART]
        for d in (4, 3, 5, 2, 6, 1, 7):
            out_send(k, d).start()
        out_in[k, c, z] = solved[k, z // 2]

    def out_pass(k):
        for d in range(1, NZ):
            out_send(k, d).wait_recv()
        out_share(k).start()

    def out_end(k):
        out_share(k).wait_recv()
        flat[...] = out_in[k].reshape(S, PART).T
        out[k] = flat[pl.ds(pl.multiple_of(((z * NC + c) % 4) * PIECE, PIECE), PIECE), :]

    multiply(2)
    pl.semaphore_wait(barrier, len(partners))
    half_send(2).start()
    pump("start")
    multiply(1)
    half_to_x(2)
    half_send(1).start()
    pump("x2")
    multiply(0)
    half_send(0).start()
    half_to_x(1)
    half_to_x(0)
    loads["noise"].wait()
    for k in range(3):
        noise_t[k] = noise_v[k].T.reshape(NZ, GROUP, PART)
    pump("tails")
    x_to_z(2)
    pump("z2")
    z_to_g(2)
    x_to_z(1)
    pump("g2")
    y_start(2, product(D2, gathered(2)))
    z_to_g(1)
    x_to_z(0)
    pump("y2")
    x_two = y_end(2)
    u_start(1, product(L21, x_two))
    out_start(2, x_two)
    r_one = gathered(1)
    z_to_g(0)
    pump("u1")
    r_one = r_one - u_end(1)
    y_start(1, product(D1, r_one))
    pump("y1")
    upd = product(L20, x_two)
    r_zero = gathered(0)
    out_pass(2)
    x_one = y_end(1)
    u_start(0, upd + product(L10, x_one))
    out_start(1, x_one)
    pump("u0")
    out_end(2)
    r_zero = r_zero - u_end(0)
    y_start(0, product(D0, r_zero))
    out_pass(1)
    x_zero = y_end(0)
    out_start(0, x_zero)
    out_end(1)
    out_pass(0)
    for k in range(3):
        half_send(k).wait_send()
        out_share(k).wait_send()
        for d in range(1, NX):
            for copy in (x_send(k, d), g_send(k, d), y_send(k, d)):
                copy.wait_send()
        for d in range(1, NZ):
            z_send(k, d).wait_send()
            out_send(k, d).wait_send()
    for k in range(2):
        for d in range(1, NX):
            u_send(k, d).wait_send()
    for m in range(6):
        c_send(m).wait_send()
        for s in range(1, 5):
            ring(m, s).wait_send()
            share(m, s).wait_send()
    out_end(0)


def local(panel, tail_samples, noise, inner, diag_inverse):
    dma = pltpu.SemaphoreType.DMA
    anywhere = pl.BlockSpec(memory_space=pl.ANY)
    return pl.pallas_call(
        kernel,
        name="substitution",
        out_shape=jax.ShapeDtypeStruct((3, PIECE, S), F32),
        in_specs=[anywhere] * 5,
        out_specs=pl.BlockSpec(memory_space=pltpu.VMEM),
        scratch_shapes=[
            pltpu.VMEM((3, ROWS, COLS), BF16),
            pltpu.VMEM((ROWS, S), BF16),
            pltpu.VMEM((S, ROWS), BF16),
            pltpu.VMEM((3, PART, PART), F32),
            pltpu.VMEM((3, NZ, GROUP, PART), F32),
            pltpu.VMEM((3, S, COLS), F32),
            pltpu.VMEM((3, PART, COLS), F32),
            pltpu.VMEM((3, NX, PART, PART), F32),
            pltpu.VMEM((3, NX, PART, PART), F32),
            pltpu.VMEM((3, NZ, GROUP, PART), F32),
            pltpu.VMEM((3, NZ, GROUP, PART), F32),
            pltpu.VMEM((3, NX, GROUP, PART), F32),
            pltpu.VMEM((6, NZ, NC, PIECE, COLS), F32),
            pltpu.VMEM((6, COLS, COLS), BF16),
            pltpu.VMEM((6, COLS, COLS), BF16),
            pltpu.VMEM((3, NY, GROUP, COLS), F32),
            pltpu.VMEM((2, NX, GROUP, COLS), F32),
            pltpu.VMEM((3, 4, GROUP, PART), F32),
            pltpu.VMEM((3, NC, NZ, GROUP, PART), F32),
            pltpu.VMEM((PART, S), F32),
            dma((13,)), dma((6,)),
            dma((3,)), dma((3,)),
            dma((3, NX - 1)), dma((3, NX - 1)),
            dma((3, NZ - 1)), dma((3, NZ - 1)),
            dma((3, NX - 1)), dma((3, NX - 1)),
            dma((6,)), dma((6,)),
            dma((6, 4)), dma((6, 4)),
            dma((6, 4)), dma((6, 4)),
            dma((3, NY - 1)), dma((3, NY - 1)),
            dma((2, NX - 1)), dma((2, NX - 1)),
            dma((3, NZ - 1)), dma((3, NZ - 1)),
            dma((3,)), dma((3,)),
        ],
        compiler_params=pltpu.CompilerParams(
            collective_id=0, has_side_effects=True, vmem_limit_bytes=56 * 2**20
        ),
    )(
        jnp.transpose(panel, (1, 0, 2)),
        tail_samples,
        noise,
        inner,
        jnp.transpose(diag_inverse, (0, 2, 1)),
    )


def solution(mesh):
    placed = (
        P("wide", None, "narrow"),
        P("wide", None),
        P(None, "narrow", None),
        P(None, "wide", "narrow"),
        P(None, "narrow", "wide"),
    )
    return jax.shard_map(
        local, mesh=mesh, in_specs=placed, out_specs=P(None, "wide", None), check_vma=False
    )
```

time: 634 us -> 74.4 us (0.12)
  waiting for transfers between devices: 556 us -> 0 us
  Pallas kernels: 0 us -> 72.8 us
  blocking collectives: 40 us -> 0 us
  matrix products: 16.1 us -> 0 us
  between operations: 13.2 us -> 0.01 us
    psum x3 -> x0, waiting for transfers between devices: 556 us -> none  [the longest x1 190 us: local(): tail_terms = lax.psum(partial_value, 'wide')]
    pallas_call x0 -> x1, Pallas kernels: none -> 72.8 us  [local(): pl.pallas_call(kernel, name='substitution', out_shape=jax.ShapeDtypeStruc...]
    psum x3 -> x0, blocking collectives: 40 us -> none  [solve_block(): return lax.psum(jnp.dot(inverse.T, remainder, precision=HI), 'narrow')]
    dot_general x7 -> x0, matrix products: 16.1 us -> none  [the longest x1 7.48 us: local(): jnp.einsum('rkj,rs->kjs', panel, tail_samples, preferred_element_type=jnp...]
  transfers between devices with their start and end apart: 3 -> 0, of which waited for: 3 -> 0; matrix products, arithmetic and copies ran while one was open for 0% -> 0% of each run, Pallas kernels for 0% -> 0%
where the time goes in v1:
time: 74.4 us; the launch traced here: 74.3 us
  Pallas kernels  72.8 us (98%)
  local copies, waits for them, and re-layouts  1.54 us (2%)
    pallas_call x1, Pallas kernels, local(): pl.pallas_call(kernel, name='substitution', out_shape=jax.ShapeDtypeStruc...  72.8 us
    unnamed x1, local copies, waits for them, and re-layouts  1.54 us

profile of v1, /device:TPU:1, one launch (start us, length us, event | category | flops | bytes accessed | tf_op | source)
XLA Modules:
  0.0 74.3 jit_solution(3313505711385507654)
XLA Ops:
  0.0 72.8 %substitution.1 = f32[3,32,256]{2,1,0:T(8,128)} custom-call(bf16[3,3072,512]{2,1,0:T(8,128)(2,1)} %bitcast.2, bf16[3072,256]{1,0:T(8,128)(2,1)} %tail.1, f32[3,512,256]{2,1,0:T(8,128)} %noise.1, f32[3,32,512]{2,1,0:T(8,128)} %inner.1, f32[3,32,512]{2,1,0:T(8,128)} %bitcast.3), custom_call_target="tpu_custom_call" | custom-call | tf_op jit(solution)/shard_map/substitution/pallas_call | solution.py:326
  72.8 1.5 %copy.7 = f32[3,32,256]{2,1,0:T(8,128)} copy(f32[3,32,256]{2,1,0:T(8,128)} %substitution.1) | data formatting | bytes 196608

commit v2 on v1

--- a/solution.py
+++ b/solution.py
@@ -13,17 +13,15 @@
 F32, BF16 = jnp.float32, jnp.bfloat16
 D2, L21, D1, L20, L10, D0 = range(6)
 SOURCE = (("d", 2), ("i", 2), ("d", 1), ("i", 1), ("i", 0), ("d", 0))
-PLAN = {
-    "start": [(m, 0) for m in range(6)],
-    "x2": [(D2, 1), (L21, 1)],
-    "tails": [(D2, 2), (D1, 1)],
-    "z2": [(L21, 2), (D2, 3)],
-    "g2": [(D2, 4), (L21, 3), (D1, 2), (L20, 1), (D2, 5), (D2, 6)],
-    "y2": [(L21, 4), (D1, 3), (L20, 2), (L10, 1), (L21, 5), (L21, 6)],
-    "u1": [(D1, 4), (L20, 3), (L10, 2), (D0, 1), (D1, 5), (D1, 6)],
-    "y1": [(L20, 4), (L10, 3), (D0, 2), (L20, 5), (L10, 4), (D0, 3), (L10, 5), (L20, 6), (L10, 6)],
-    "u0": [(D0, 4), (D0, 5), (D0, 6)],
-}
+FLOW = (
+    "mul 2", "enter", "half 2", "b 0 0", "b 1 0", "b 2 0", "b 3 0", "b 4 0", "b 5 0", "mul 1", "x 2", "b 0 1", "b 1 1",
+    "half 1", "mul 0", "b 2 1", "half 0", "x 1", "b 3 1", "noise", "x 0", "b 0 2", "z 2", "b 1 2", "b 2 2", "z 1",
+    "b 0 3", "z 0", "g 2", "b 1 3", "b 2 3", "b 0 4", "g 1", "b 3 2", "b 1 4", "b 4 1", "g 0", "b 0 5", "b 2 4",
+    "b 5 1", "b 0 6", "solve 2", "b 1 5", "b 3 3", "b 4 2", "b 2 5", "b 1 6", "b 5 2", "b 2 6", "b 3 4", "update 1",
+    "b 4 3", "out 2", "b 5 3", "b 3 5", "b 4 4", "b 3 6", "solve 1", "pre", "b 5 4", "b 4 5", "pass 2", "b 4 6",
+    "b 5 5", "update 0", "out 1", "b 5 6", "write 2", "solve 0", "pass 1", "out 0", "write 1", "pass 0", "drain",
+    "write 0",
+)
 
 
 def halves(a):
@@ -44,10 +42,23 @@
     def at(z_to, x_to, c_to, y_to):
         return ((z_to * NX + x_to) * NC + c_to, y_to)
 
-    def send(src, dst, send_sem, recv_sem, to):
-        return pltpu.make_async_remote_copy(
-            src_ref=src, dst_ref=dst, send_sem=send_sem, recv_sem=recv_sem, device_id=to, device_id_type=MESH
-        )
+    started, open_in = {}, {}
+
+    class send:
+        def __init__(self, src, dst, send_sem, recv_sem, to, key=None):
+            self.copy = pltpu.make_async_remote_copy(
+                src_ref=src, dst_ref=dst, send_sem=send_sem, recv_sem=recv_sem, device_id=to, device_id_type=MESH
+            )
+            self.key = key
+
+        def start(self):
+            self.copy.start()
+            started[self.key] = self.copy
+            open_in[self.key] = self.copy
+
+        def wait_recv(self):
+            self.copy.wait_recv()
+            del open_in[self.key]
 
     def zp(k):
         return (z + k + 2 * NZ) % NZ
@@ -108,16 +119,16 @@
                 part_t[k] += term
 
     def half_send(k):
-        return send(part_t.at[k, pl.ds(pl.multiple_of((1 - c) * PART, PART), PART)], half_in.at[k], hs.at[k], hr.at[k], mate)
+        return send(part_t.at[k, pl.ds(pl.multiple_of((1 - c) * PART, PART), PART)], half_in.at[k], hs.at[k], hr.at[k], mate, ("half_send", k))
 
     def x_send(k, d):
-        return send(half_sum.at[k, xp(d)], x_in.at[k, x], xs.at[k, d - 1], xr.at[k, d - 1], at(z, xp(d), c, y))
+        return send(half_sum.at[k, xp(d)], x_in.at[k, x], xs.at[k, d - 1], xr.at[k, d - 1], at(z, xp(d), c, y), ("x_send", k, d))
 
     def z_send(k, d):
-        return send(z_sum.at[k, zp(d)], z_in.at[k, z], zs.at[k, d - 1], zr.at[k, d - 1], at(zp(d), x, c, y))
+        return send(z_sum.at[k, zp(d)], z_in.at[k, z], zs.at[k, d - 1], zr.at[k, d - 1], at(zp(d), x, c, y), ("z_send", k, d))
 
     def g_send(k, d):
-        return send(right.at[k, x], right.at[k, x], gs.at[k, d - 1], gr.at[k, d - 1], at(z, xp(d), c, y))
+        return send(right.at[k, x], right.at[k, x], gs.at[k, d - 1], gr.at[k, d - 1], at(z, xp(d), c, y), ("g_send", k, d))
 
     def half_to_x(k):
         half_send(k).wait_recv()
@@ -153,18 +164,18 @@
         return jnp.concatenate([right[k, i] for i in range(NX)], axis=1)
 
     def c_send(m):
-        return send(grid.at[m, z, c], grid.at[m, z, c], cs.at[m], cr.at[m], mate)
+        return send(grid.at[m, z, c], grid.at[m, z, c], cs.at[m], cr.at[m], mate, ("c_send", m))
 
     def ring(m, s):
         if s < 4:
             piece = grid.at[m, zp(-(s - 1) * way)]
         else:
             piece = grid.at[m, zp(-3 * way), c]
-        return send(piece, piece, rs.at[m, s - 1], rr.at[m, s - 1], at(zp(way), x, c, y))
+        return send(piece, piece, rs.at[m, s - 1], rr.at[m, s - 1], at(zp(way), x, c, y), ("ring", m, s))
 
     def share(m, s):
         piece = grid.at[m, zp(-s * way)] if s < 4 else grid.at[m, zp(-4 * way), c]
-        return send(piece, piece, ss.at[m, s - 1], sr.at[m, s - 1], mate)
+        return send(piece, piece, ss.at[m, s - 1], sr.at[m, s - 1], mate, ("share", m, s))
 
     def step(m, s):
         if s == 0:
@@ -188,10 +199,6 @@
                 rows = slice(q * COLS // 2, (q + 1) * COLS // 2)
                 high[m, rows], low[m, rows] = halves(grid[m, zs_].reshape(COLS // 2, COLS))
 
-    def pump(point):
-        for m, s in PLAN[point]:
-            step(m, s)
-
     def product(m, vector):
         dims = (((1,), (1,)), ((), ())) if SOURCE[m][0] == "d" else (((1,), (0,)), ((), ()))
         v_high, v_low = halves(vector)
@@ -200,7 +207,7 @@
         return both[:GROUP] + both[GROUP:] + rest
 
     def y_send(k, d):
-        return send(y_buf.at[k, y], y_buf.at[k, y], ys.at[k, d - 1], yr.at[k, d - 1], at(z, x, c, yp(d)))
+        return send(y_buf.at[k, y], y_buf.at[k, y], ys.at[k, d - 1], yr.at[k, d - 1], at(z, x, c, yp(d)), ("y_send", k, d))
 
     def y_start(k, term):
         y_buf[k, y] = term
@@ -214,7 +221,7 @@
         return total
 
     def u_send(k, d):
-        return send(u_buf.at[k, x], u_buf.at[k, x], us.at[k, d - 1], ur.at[k, d - 1], at(z, xp(d), c, y))
+        return send(u_buf.at[k, x], u_buf.at[k, x], us.at[k, d - 1], ur.at[k, d - 1], at(z, xp(d), c, y), ("u_send", k, d))
 
     def u_start(k, term):
         u_buf[k, x] = term
@@ -227,12 +234,10 @@
         return (u_buf[k, 0] + u_buf[k, 1]) + (u_buf[k, 2] + u_buf[k, 3])
 
     def out_send(k, d):
-        return send(
-            solved.at[k, zp(d) // 2], out_in.at[k, c, z], os.at[k, d - 1], orr.at[k, d - 1], at(zp(d), x, c, y)
-        )
+        return send(solved.at[k, zp(d) // 2], out_in.at[k, c, z], os.at[k, d - 1], orr.at[k, d - 1], at(zp(d), x, c, y), ("out_send", k, d))
 
     def out_share(k):
-        return send(out_in.at[k, c], out_in.at[k, c], ps.at[k], pr.at[k], mate)
+        return send(out_in.at[k, c], out_in.at[k, c], ps.at[k], pr.at[k], mate, ("out_share", k))
 
     def out_start(k, vector):
         for i in range(NX):
@@ -251,73 +256,49 @@
         flat[...] = out_in[k].reshape(S, PART).T
         out[k] = flat[pl.ds(pl.multiple_of(((z * NC + c) % 4) * PIECE, PIECE), PIECE), :]
 
-    multiply(2)
-    pl.semaphore_wait(barrier, len(partners))
-    half_send(2).start()
-    pump("start")
-    multiply(1)
-    half_to_x(2)
-    half_send(1).start()
-    pump("x2")
-    multiply(0)
-    half_send(0).start()
-    half_to_x(1)
-    half_to_x(0)
-    loads["noise"].wait()
-    for k in range(3):
-        noise_t[k] = noise_v[k].T.reshape(NZ, GROUP, PART)
-    pump("tails")
-    x_to_z(2)
-    pump("z2")
-    z_to_g(2)
-    x_to_z(1)
-    pump("g2")
-    y_start(2, product(D2, gathered(2)))
-    z_to_g(1)
-    x_to_z(0)
-    pump("y2")
-    x_two = y_end(2)
-    u_start(1, product(L21, x_two))
-    out_start(2, x_two)
-    r_one = gathered(1)
-    z_to_g(0)
-    pump("u1")
-    r_one = r_one - u_end(1)
-    y_start(1, product(D1, r_one))
-    pump("y1")
-    upd = product(L20, x_two)
-    r_zero = gathered(0)
-    out_pass(2)
-    x_one = y_end(1)
-    u_start(0, upd + product(L10, x_one))
-    out_start(1, x_one)
-    pump("u0")
-    out_end(2)
-    r_zero = r_zero - u_end(0)
-    y_start(0, product(D0, r_zero))
-    out_pass(1)
-    x_zero = y_end(0)
-    out_start(0, x_zero)
-    out_end(1)
-    out_pass(0)
-    for k in range(3):
-        half_send(k).wait_send()
-        out_share(k).wait_send()
-        for d in range(1, NX):
-            for copy in (x_send(k, d), g_send(k, d), y_send(k, d)):
-                copy.wait_send()
-        for d in range(1, NZ):
-            z_send(k, d).wait_send()
-            out_send(k, d).wait_send()
-    for k in range(2):
-        for d in range(1, NX):
-            u_send(k, d).wait_send()
-    for m in range(6):
-        c_send(m).wait_send()
-        for s in range(1, 5):
-            ring(m, s).wait_send()
-            share(m, s).wait_send()
-    out_end(0)
+    kept = {}
+
+    def enter():
+        pl.semaphore_wait(barrier, len(partners))
+
+    def noise_turn():
+        loads["noise"].wait()
+        for k in range(3):
+            noise_t[k] = noise_v[k].T.reshape(NZ, GROUP, PART)
+
+    def solve(k):
+        value = gathered(k)
+        if k < 2:
+            value = value - u_end(k)
+        y_start(k, product((D0, D1, D2)[k], value))
+
+    def update(k):
+        kept[k + 1] = y_end(k + 1)
+        if k == 1:
+            u_start(1, product(L21, kept[2]))
+        else:
+            u_start(0, kept["pre"] + product(L10, kept[1]))
+
+    def pre():
+        kept["pre"] = product(L20, kept[2])
+
+    def to_out(k):
+        if k == 0:
+            kept[0] = y_end(0)
+        out_start(k, kept[k])
+
+    def drain():
+        for copy in started.values():
+            copy.wait_send()
+
+    work = {
+        "mul": multiply, "enter": enter, "half": lambda k: half_send(k).start(), "b": step, "x": half_to_x, "noise": noise_turn,
+        "z": x_to_z, "g": z_to_g, "solve": solve, "update": update, "pre": pre, "out": to_out, "pass": out_pass,
+        "write": out_end, "drain": drain,
+    }
+    for entry in FLOW:
+        name, *numbers = entry.split()
+        work[name](*map(int, numbers))
 
 
 def local(panel, tail_samples, noise, inner, diag_inverse):

time: 74.4 us -> 71.2 us (0.957)
  Pallas kernels: 72.8 us -> 69.5 us
    pallas_call x1, Pallas kernels: 72.8 us -> 69.5 us  [local(): pl.pallas_call(kernel, name='substitution', out_shape=jax.ShapeDtypeStruc...]
where the time goes in v2:
time: 71.2 us; the launch traced here: 71.1 us
  Pallas kernels  69.5 us (98%)
  local copies, waits for them, and re-layouts  1.54 us (2%)
    pallas_call x1, Pallas kernels, local(): pl.pallas_call(kernel, name='substitution', out_shape=jax.ShapeDtypeStruc...  69.5 us
    unnamed x1, local copies, waits for them, and re-layouts  1.54 us

profile of v2, /device:TPU:1, one launch (start us, length us, event | category | flops | bytes accessed | tf_op | source)
XLA Modules:
  0.0 71.1 jit_solution(15124861828304544794)
XLA Ops:
  0.0 69.5 %substitution.1 = f32[3,32,256]{2,1,0:T(8,128)} custom-call(bf16[3,3072,512]{2,1,0:T(8,128)(2,1)} %bitcast.2, bf16[3072,256]{1,0:T(8,128)(2,1)} %tail.1, f32[3,512,256]{2,1,0:T(8,128)} %noise.1, f32[3,32,512]{2,1,0:T(8,128)} %inner.1, f32[3,32,512]{2,1,0:T(8,128)} %bitcast.3), custom_call_target="tpu_custom_call" | custom-call | tf_op jit(solution)/shard_map/substitution/pallas_call | solution.py:307
  69.5 1.5 %copy.7 = f32[3,32,256]{2,1,0:T(8,128)} copy(f32[3,32,256]{2,1,0:T(8,128)} %substitution.1) | data formatting | bytes 196608

commit v3 on v2

--- a/solution.py
+++ b/solution.py
@@ -16,9 +16,9 @@
 FLOW = (
     "mul 2", "enter", "half 2", "b 0 0", "b 1 0", "b 2 0", "b 3 0", "b 4 0", "b 5 0", "mul 1", "x 2", "b 0 1", "b 1 1",
     "half 1", "mul 0", "b 2 1", "half 0", "x 1", "b 3 1", "noise", "x 0", "b 0 2", "z 2", "b 1 2", "b 2 2", "z 1",
-    "b 0 3", "z 0", "g 2", "b 1 3", "b 2 3", "b 0 4", "g 1", "b 3 2", "b 1 4", "b 4 1", "g 0", "b 0 5", "b 2 4",
-    "b 5 1", "b 0 6", "solve 2", "b 1 5", "b 3 3", "b 4 2", "b 2 5", "b 1 6", "b 5 2", "b 2 6", "b 3 4", "update 1",
-    "b 4 3", "out 2", "b 5 3", "b 3 5", "b 4 4", "b 3 6", "solve 1", "pre", "b 5 4", "b 4 5", "pass 2", "b 4 6",
+    "b 0 3", "z 0", "g 2", "b 1 3", "b 2 3", "b 0 4", "g 1", "b 3 2", "b 4 1", "g 0", "b 1 4", "b 2 4", "b 0 5",
+    "b 5 1", "b 0 6", "solve 2", "b 3 3", "b 4 2", "b 1 5", "b 2 5", "b 1 6", "b 5 2", "b 2 6", "b 3 4", "update 1",
+    "b 4 3", "out 2", "b 5 3", "b 3 5", "b 3 6", "b 4 4", "solve 1", "pre", "b 5 4", "b 4 5", "pass 2", "b 4 6",
     "b 5 5", "update 0", "out 1", "b 5 6", "write 2", "solve 0", "pass 1", "out 0", "write 1", "pass 0", "drain",
     "write 0",
 )

time: 71.2 us -> 71.2 us (level)
  no operation moved by 1% of the time
where the time goes in v3:
time: 71.2 us; the launch traced here: 71.1 us
  Pallas kernels  69.5 us (98%)
  local copies, waits for them, and re-layouts  1.54 us (2%)
    pallas_call x1, Pallas kernels, local(): pl.pallas_call(kernel, name='substitution', out_shape=jax.ShapeDtypeStruc...  69.5 us
    unnamed x1, local copies, waits for them, and re-layouts  1.54 us

profile of v3, /device:TPU:1, one launch (start us, length us, event | category | flops | bytes accessed | tf_op | source)
XLA Modules:
  0.0 71.1 jit_solution(9850956794014885200)
XLA Ops:
  0.0 69.5 %substitution.1 = f32[3,32,256]{2,1,0:T(8,128)} custom-call(bf16[3,3072,512]{2,1,0:T(8,128)(2,1)} %bitcast.2, bf16[3072,256]{1,0:T(8,128)(2,1)} %tail.1, f32[3,512,256]{2,1,0:T(8,128)} %noise.1, f32[3,32,512]{2,1,0:T(8,128)} %inner.1, f32[3,32,512]{2,1,0:T(8,128)} %bitcast.3), custom_call_target="tpu_custom_call" | custom-call | tf_op jit(solution)/shard_map/substitution/pallas_call | solution.py:307
  69.5 1.5 %copy.7 = f32[3,32,256]{2,1,0:T(8,128)} copy(f32[3,32,256]{2,1,0:T(8,128)} %substitution.1) | data formatting | bytes 196608
